TPU v7x, 32 devices: a whole 2x2x4 slice. The times are simulated.
32 devices in a mesh: dp: 16 (over z, y, core), mp: 2 (over x).
Axes of the slice: x: 2, y: 2, z: 4, core: 2. Of those that a mesh axis runs over, the one named last changes fastest.
Arguments:
- views: bfloat16 [8192, 256], P('dp'), may hold values from -1 to 1
- partner: int32 [8192], P('dp'), may hold values from 0 to 8191, as said below
- weight: float32 [8192], P('dp'), may hold values from 0.25 to 4
Outputs:
- loss: float32 [8192], P('dp')
- grad: float32 [8192, 256], P('dp')
Inputs may be any that keep to these rules, and one draw needn't show every extreme that they name: partner pairs the views: partner[partner[i]] = i and partner[i] != i.
All inputs are finite; a program needn't handle non-finite values.
Results may differ from a plain program's by a relative error of at most 0.0056.
Values may be sent and summed in bfloat16 or wider, within the bound.
A program may use at most 64 MiB of HBM per device.

v0:
```python
import jax
import jax.numpy as jnp
from jax import lax
from jax.sharding import PartitionSpec as P

INV_TAU = 10.0
EPS = 1e-06


def shards(views, partner, weight):
    rows_dev = views.shape[0]
    width = views.shape[1]
    parts = lax.axis_size("mp")
    slot = lax.axis_index("mp")
    block_index = lax.axis_index("dp")
    piece = rows_dev // parts
    floats = views.astype(jnp.float32)
    length = jnp.sqrt(jnp.sum(floats * floats, axis=1) + EPS)
    unit = floats / length[:, None]
    normal = unit.astype(jnp.bfloat16)
    offset = slot * piece
    mine = lax.dynamic_slice_in_dim(normal, offset, piece, 0)
    columns = lax.all_gather(mine, "dp", axis=0, tiled=True)
    width_cols = columns.shape[0]
    step_cols = min(512, width_cols)
    count = width_cols // step_cols
    position = jnp.arange(width_cols, dtype=jnp.int32)
    col_ids = position // piece * rows_dev + offset + position % piece
    row_ids = block_index * rows_dev + jnp.arange(rows_dev, dtype=jnp.int32)
    id_blocks = col_ids.reshape(count, step_cols)

    def tile(cols_block, ids_block):
        s = (
            lax.dot_general(
                normal, cols_block, (((1,), (1,)), ((), ())), preferred_element_type=jnp.float32
            )
            * INV_TAU
        )
        off = row_ids[:, None] != ids_block[None, :]
        match = partner[:, None] == ids_block[None, :]
        return (s, off, match)

    def forward(carry, inputs):
        cols_block, ids_block = inputs
        s, off, match = tile(cols_block, ids_block)
        total = carry[0] + jnp.sum(jnp.where(off, jnp.exp(s), jnp.float32(0.0)), axis=1)
        positive = carry[1] + jnp.sum(jnp.where(match, s, jnp.float32(0.0)), axis=1)
        return ((total, positive), None)

    zeros_rows = jnp.zeros((rows_dev,), jnp.float32)
    col_blocks = columns.reshape(count, step_cols, width)
    (total, positive), _ = lax.scan(forward, (zeros_rows, zeros_rows), (col_blocks, id_blocks))
    total, positive = lax.psum((total, positive), "mp")
    lse = jnp.log(total)
    loss = lse - positive
    lse_mine = lax.dynamic_slice_in_dim(lse, offset, piece, 0)
    weight_mine = lax.dynamic_slice_in_dim(weight, offset, piece, 0)
    col_lse, col_weight = (
        lax.all_gather(lse_mine, "dp", axis=0, tiled=True),
        lax.all_gather(weight_mine, "dp", axis=0, tiled=True),
    )

    def backward(acc, inputs):
        cols_block, ids_block, lse_block, weight_block = inputs
        s, off, match = tile(cols_block, ids_block)
        prow = jnp.exp(s - lse[:, None])
        pcol = jnp.exp(s - lse_block[None, :])
        coef = jnp.where(
            off, weight[:, None] * prow + weight_block[None, :] * pcol, jnp.float32(0.0)
        )
        coef = coef - jnp.where(match, weight[:, None] + weight_block[None, :], jnp.float32(0.0))
        coef = coef.astype(jnp.bfloat16)
        return (acc + jnp.dot(coef, cols_block, preferred_element_type=jnp.float32), None)

    start_acc = jnp.zeros((rows_dev, width), jnp.float32)
    partial_grad, _ = lax.scan(
        backward,
        start_acc,
        (
            col_blocks,
            id_blocks,
            col_lse.reshape(count, step_cols),
            col_weight.reshape(count, step_cols),
        ),
    )
    share = lax.psum_scatter(partial_grad, "mp", scatter_dimension=0, tiled=True) * INV_TAU
    unit_share = lax.dynamic_slice_in_dim(unit, offset, piece, 0)
    length_share = lax.dynamic_slice_in_dim(length, offset, piece, 0)
    finished = (
        share - unit_share * jnp.sum(unit_share * share, axis=1, keepdims=True)
    ) / length_share[:, None]
    grad = lax.all_gather(finished, "mp", axis=0, tiled=True)
    return (loss, grad)


def solution(mesh):
    return jax.shard_map(
        shards,
        mesh=mesh,
        in_specs=(P("dp", None), P("dp"), P("dp")),
        out_specs=(P("dp"), P("dp", None)),
        check_vma=False,
    )
```

profile of v0, /device:TPU:0, one launch (start us, length us, event | category | flops | bytes accessed | tf_op | source)
XLA Modules:
  0.0 140.7 jit_solution(16877121199656631432)
XLA Ops:
  7.2 0.0 all-gather.4.cloned.1.call-start
  7.2 1.1 fusion.31
  8.3 1.1 convert_divide_fusion
  9.4 0.7 constant_dynamic-slice_fusion.4
  10.1 0.0 all-gather.4.cloned.1.call-update
  10.1 0.0 reduce-scatter.2.cloned.1.call-start
  10.2 0.8 dynamic_slice.37
  11.0 23.1 %all-gather = f32[16,1,256]{2,1,0:T(1,128)S(1)} all-gather(f32[1,1,256]{2,1,0:T(1,128)S(1)} %bitcast.52), channel_id=1, replica_groups=mesh['dp'=16,'mp'=2] {'dp'}, dimensions={0}, use_global_device_ids=true | all-gather | bytes 17408 | tf_op jit(solution)/shard_map/all_gather | solution.py:60
  34.2 20.7 %all-gather.4.cloned.1.call-done = bf16[4096,256]{1,0:T(8,128)(2,1)} async-done(((bf16[256,256]{1,0:T(8,128)(2,1)}), bf16[4096,256]{1,0:T(8,128)(2,1)}) %all-gather.4.cloned.1.call-update) | async-done | bytes 2097168 | tf_op jit(solution)/shard_map/all_gather | solution.py:23
  54.9 0.0 copy-start.1
  54.9 12.3 %while.24 = (s32[]{:T(128)}, f32[512]{0:T(512)S(1)}, f32[512]{0:T(512)S(1)}, s32[8,512]{1,0:T(8,128)S(1)}, bf16[8,512,256]{2,1,0:T(8,128)(2,1)}, /*index=5*/bf16...) while((s32[]{:T(128)}, f32[512]{0:T(512)S(1)}, f32[512]{0:T(512)S(1)}, ...), condition=%wide.region_4.5_spmd.clone, body=%wide.region_1.4_spmd.clone.sunk | while | flops 136054272 | bytes 553091 | solution.py:52
  54.9 1.5 %select_reduce_fusion.3 = (f32[512]{0:T(512)S(1)}, f32[512]{0:T(512)S(1)}) fusion(s32[512]{0:T(512)} %get-tuple-element.378, s32[512]{0:T(512)S(1)} %bitcast.51, s32[512]{0:T(512)S(1)} %iota_add_fusion.4, bf16[512,256]{1,0:T(8,128)(2,1)S(1)} %get-tuple-element.377, bf16[8,512,256]{2,1,0:T(8,128)(2,1)} %get-tuple-element.376, s32[]{:T(128)S(6)} %copy.8), kind=kOutput, calls=%fused_computation.4.clone.1 | convolution fusion | flops 136051712 | bytes 534532 | tf_op jit(solution)/shard_map/while/body/eval_jaxpr/dot_general | solution.py:34
  56.4 1.5 %select_reduce_fusion.3 = (f32[512]{0:T(512)S(1)}, f32[512]{0:T(512)S(1)}) fusion(s32[512]{0:T(512)} %get-tuple-element.378, s32[512]{0:T(512)S(1)} %bitcast.51, s32[512]{0:T(512)S(1)} %iota_add_fusion.4, bf16[512,256]{1,0:T(8,128)(2,1)S(1)} %get-tuple-element.377, bf16[8,512,256]{2,1,0:T(8,128)(2,1)} %get-tuple-element.376, s32[]{:T(128)S(6)} %copy.8), kind=kOutput, calls=%fused_computation.4.clone.1 | convolution fusion | flops 136051712 | bytes 534532 | tf_op jit(solution)/shard_map/while/body/eval_jaxpr/dot_general | solution.py:34
  58.0 1.5 %select_reduce_fusion.3 = (f32[512]{0:T(512)S(1)}, f32[512]{0:T(512)S(1)}) fusion(s32[512]{0:T(512)} %get-tuple-element.378, s32[512]{0:T(512)S(1)} %bitcast.51, s32[512]{0:T(512)S(1)} %iota_add_fusion.4, bf16[512,256]{1,0:T(8,128)(2,1)S(1)} %get-tuple-element.377, bf16[8,512,256]{2,1,0:T(8,128)(2,1)} %get-tuple-element.376, s32[]{:T(128)S(6)} %copy.8), kind=kOutput, calls=%fused_computation.4.clone.1 | convolution fusion | flops 136051712 | bytes 534532 | tf_op jit(solution)/shard_map/while/body/eval_jaxpr/dot_general | solution.py:34
  59.5 1.5 %select_reduce_fusion.3 = (f32[512]{0:T(512)S(1)}, f32[512]{0:T(512)S(1)}) fusion(s32[512]{0:T(512)} %get-tuple-element.378, s32[512]{0:T(512)S(1)} %bitcast.51, s32[512]{0:T(512)S(1)} %iota_add_fusion.4, bf16[512,256]{1,0:T(8,128)(2,1)S(1)} %get-tuple-element.377, bf16[8,512,256]{2,1,0:T(8,128)(2,1)} %get-tuple-element.376, s32[]{:T(128)S(6)} %copy.8), kind=kOutput, calls=%fused_computation.4.clone.1 | convolution fusion | flops 136051712 | bytes 534532 | tf_op jit(solution)/shard_map/while/body/eval_jaxpr/dot_general | solution.py:34
  61.1 1.5 %select_reduce_fusion.3 = (f32[512]{0:T(512)S(1)}, f32[512]{0:T(512)S(1)}) fusion(s32[512]{0:T(512)} %get-tuple-element.378, s32[512]{0:T(512)S(1)} %bitcast.51, s32[512]{0:T(512)S(1)} %iota_add_fusion.4, bf16[512,256]{1,0:T(8,128)(2,1)S(1)} %get-tuple-element.377, bf16[8,512,256]{2,1,0:T(8,128)(2,1)} %get-tuple-element.376, s32[]{:T(128)S(6)} %copy.8), kind=kOutput, calls=%fused_computation.4.clone.1 | convolution fusion | flops 136051712 | bytes 534532 | tf_op jit(solution)/shard_map/while/body/eval_jaxpr/dot_general | solution.py:34
  62.6 1.5 %select_reduce_fusion.3 = (f32[512]{0:T(512)S(1)}, f32[512]{0:T(512)S(1)}) fusion(s32[512]{0:T(512)} %get-tuple-element.378, s32[512]{0:T(512)S(1)} %bitcast.51, s32[512]{0:T(512)S(1)} %iota_add_fusion.4, bf16[512,256]{1,0:T(8,128)(2,1)S(1)} %get-tuple-element.377, bf16[8,512,256]{2,1,0:T(8,128)(2,1)} %get-tuple-element.376, s32[]{:T(128)S(6)} %copy.8), kind=kOutput, calls=%fused_computation.4.clone.1 | convolution fusion | flops 136051712 | bytes 534532 | tf_op jit(solution)/shard_map/while/body/eval_jaxpr/dot_general | solution.py:34
  64.1 1.5 %select_reduce_fusion.3 = (f32[512]{0:T(512)S(1)}, f32[512]{0:T(512)S(1)}) fusion(s32[512]{0:T(512)} %get-tuple-element.378, s32[512]{0:T(512)S(1)} %bitcast.51, s32[512]{0:T(512)S(1)} %iota_add_fusion.4, bf16[512,256]{1,0:T(8,128)(2,1)S(1)} %get-tuple-element.377, bf16[8,512,256]{2,1,0:T(8,128)(2,1)} %get-tuple-element.376, s32[]{:T(128)S(6)} %copy.8), kind=kOutput, calls=%fused_computation.4.clone.1 | convolution fusion | flops 136051712 | bytes 534532 | tf_op jit(solution)/shard_map/while/body/eval_jaxpr/dot_general | solution.py:34
  65.7 1.5 %select_reduce_fusion.3 = (f32[512]{0:T(512)S(1)}, f32[512]{0:T(512)S(1)}) fusion(s32[512]{0:T(512)} %get-tuple-element.378, s32[512]{0:T(512)S(1)} %bitcast.51, s32[512]{0:T(512)S(1)} %iota_add_fusion.4, bf16[512,256]{1,0:T(8,128)(2,1)S(1)} %get-tuple-element.377, bf16[8,512,256]{2,1,0:T(8,128)(2,1)} %get-tuple-element.376, s32[]{:T(128)S(6)} %copy.8), kind=kOutput, calls=%fused_computation.4.clone.1 | convolution fusion | flops 136051712 | bytes 534532 | tf_op jit(solution)/shard_map/while/body/eval_jaxpr/dot_general | solution.py:34
  67.2 4.9 %all-reduce = (f32[512]{0:T(512)S(1)}, f32[512]{0:T(512)S(1)}) all-reduce(f32[512]{0:T(512)S(1)} %get-tuple-element.103, f32[512]{0:T(512)S(1)} %get-tuple-element.102), channel_id=1, replica_groups=mesh['dp'=16,'mp'=2] {'mp'}, use_global_device_ids=true, to_apply=%region_6.7 | all-reduce | flops 1024 | bytes 8192 | tf_op jit(solution)/shard_map/psum | solution.py:53
  72.1 0.6 fusion.41
  72.7 0.1 dynamic_slice.38
  72.8 19.2 %all-gather.1 = f32[16,1,256]{2,1,0:T(1,128)S(1)} all-gather(f32[1,1,256]{2,1,0:T(1,128)S(1)} %bitcast.53), channel_id=1, replica_groups=mesh['dp'=16,'mp'=2] {'dp'}, dimensions={0}, use_global_device_ids=true | all-gather | bytes 17408 | tf_op jit(solution)/shard_map/all_gather | solution.py:59
  92.0 0.0 copy-done.1
  92.0 17.4 %while.25 = (s32[]{:T(128)}, f32[512,256]{1,0:T(8,128)S(1)}, s32[8,512]{1,0:T(8,128)S(1)}, f32[512]{0:T(512)S(1)}, bf16[8,512,256]{2,1,0:T(8,128)(2,1)}, /*index...) while((s32[]{:T(128)}, f32[512,256]{1,0:T(8,128)S(1)}, ...), condition=%wide.region_8.9_spmd.clone, body=%wide.region_7.8_spmd.clone.sunk | while | flops 272105984 | bytes 1869466 | solution.py:76
  92.1 2.1 %convolution_add_fusion.2 = f32[512,256]{1,0:T(8,128)S(1)} fusion(bf16[512,256]{1,0:T(8,128)(2,1)S(1)} %get-tuple-element.413, f32[512,256]{1,0:T(8,128)S(1)} %get-tuple-element.396, f32[512]{0:T(512)S(1)} %bitcast.49, f32[512]{0:T(512)S(1)} %get-tuple-element.411, s32[512]{0:T(512)} %get-tuple-element.417, f32[512]{0:T(512)S(1)} %bitcast.48, ...), kind=kOutput, calls=%fused_computation.14.clone.1 | convolution fusion | flops 272105472 | bytes 1854976 | tf_op jit(solution)/shard_map/while/body/eval_jaxpr/dot_general | solution.py:73
  94.3 2.1 %convolution_add_fusion.2 = f32[512,256]{1,0:T(8,128)S(1)} fusion(bf16[512,256]{1,0:T(8,128)(2,1)S(1)} %get-tuple-element.413, f32[512,256]{1,0:T(8,128)S(1)} %get-tuple-element.396, f32[512]{0:T(512)S(1)} %bitcast.49, f32[512]{0:T(512)S(1)} %get-tuple-element.411, s32[512]{0:T(512)} %get-tuple-element.417, f32[512]{0:T(512)S(1)} %bitcast.48, ...), kind=kOutput, calls=%fused_computation.14.clone.1 | convolution fusion | flops 272105472 | bytes 1854976 | tf_op jit(solution)/shard_map/while/body/eval_jaxpr/dot_general | solution.py:73
  96.5 2.1 %convolution_add_fusion.2 = f32[512,256]{1,0:T(8,128)S(1)} fusion(bf16[512,256]{1,0:T(8,128)(2,1)S(1)} %get-tuple-element.413, f32[512,256]{1,0:T(8,128)S(1)} %get-tuple-element.396, f32[512]{0:T(512)S(1)} %bitcast.49, f32[512]{0:T(512)S(1)} %get-tuple-element.411, s32[512]{0:T(512)} %get-tuple-element.417, f32[512]{0:T(512)S(1)} %bitcast.48, ...), kind=kOutput, calls=%fused_computation.14.clone.1 | convolution fusion | flops 272105472 | bytes 1854976 | tf_op jit(solution)/shard_map/while/body/eval_jaxpr/dot_general | solution.py:73
  98.6 2.1 %convolution_add_fusion.2 = f32[512,256]{1,0:T(8,128)S(1)} fusion(bf16[512,256]{1,0:T(8,128)(2,1)S(1)} %get-tuple-element.413, f32[512,256]{1,0:T(8,128)S(1)} %get-tuple-element.396, f32[512]{0:T(512)S(1)} %bitcast.49, f32[512]{0:T(512)S(1)} %get-tuple-element.411, s32[512]{0:T(512)} %get-tuple-element.417, f32[512]{0:T(512)S(1)} %bitcast.48, ...), kind=kOutput, calls=%fused_computation.14.clone.1 | convolution fusion | flops 272105472 | bytes 1854976 | tf_op jit(solution)/shard_map/while/body/eval_jaxpr/dot_general | solution.py:73
  100.8 2.1 %convolution_add_fusion.2 = f32[512,256]{1,0:T(8,128)S(1)} fusion(bf16[512,256]{1,0:T(8,128)(2,1)S(1)} %get-tuple-element.413, f32[512,256]{1,0:T(8,128)S(1)} %get-tuple-element.396, f32[512]{0:T(512)S(1)} %bitcast.49, f32[512]{0:T(512)S(1)} %get-tuple-element.411, s32[512]{0:T(512)} %get-tuple-element.417, f32[512]{0:T(512)S(1)} %bitcast.48, ...), kind=kOutput, calls=%fused_computation.14.clone.1 | convolution fusion | flops 272105472 | bytes 1854976 | tf_op jit(solution)/shard_map/while/body/eval_jaxpr/dot_general | solution.py:73
  103.0 2.1 %convolution_add_fusion.2 = f32[512,256]{1,0:T(8,128)S(1)} fusion(bf16[512,256]{1,0:T(8,128)(2,1)S(1)} %get-tuple-element.413, f32[512,256]{1,0:T(8,128)S(1)} %get-tuple-element.396, f32[512]{0:T(512)S(1)} %bitcast.49, f32[512]{0:T(512)S(1)} %get-tuple-element.411, s32[512]{0:T(512)} %get-tuple-element.417, f32[512]{0:T(512)S(1)} %bitcast.48, ...), kind=kOutput, calls=%fused_computation.14.clone.1 | convolution fusion | flops 272105472 | bytes 1854976 | tf_op jit(solution)/shard_map/while/body/eval_jaxpr/dot_general | solution.py:73
  105.2 2.1 %convolution_add_fusion.2 = f32[512,256]{1,0:T(8,128)S(1)} fusion(bf16[512,256]{1,0:T(8,128)(2,1)S(1)} %get-tuple-element.413, f32[512,256]{1,0:T(8,128)S(1)} %get-tuple-element.396, f32[512]{0:T(512)S(1)} %bitcast.49, f32[512]{0:T(512)S(1)} %get-tuple-element.411, s32[512]{0:T(512)} %get-tuple-element.417, f32[512]{0:T(512)S(1)} %bitcast.48, ...), kind=kOutput, calls=%fused_computation.14.clone.1 | convolution fusion | flops 272105472 | bytes 1854976 | tf_op jit(solution)/shard_map/while/body/eval_jaxpr/dot_general | solution.py:73
  107.3 2.1 %convolution_add_fusion.2 = f32[512,256]{1,0:T(8,128)S(1)} fusion(bf16[512,256]{1,0:T(8,128)(2,1)S(1)} %get-tuple-element.413, f32[512,256]{1,0:T(8,128)S(1)} %get-tuple-element.396, f32[512]{0:T(512)S(1)} %bitcast.49, f32[512]{0:T(512)S(1)} %get-tuple-element.411, s32[512]{0:T(512)} %get-tuple-element.417, f32[512]{0:T(512)S(1)} %bitcast.48, ...), kind=kOutput, calls=%fused_computation.14.clone.1 | convolution fusion | flops 272105472 | bytes 1854976 | tf_op jit(solution)/shard_map/while/body/eval_jaxpr/dot_general | solution.py:73
  109.4 0.0 copy-start
  109.5 0.8 copy-done
  110.2 0.0 reduce-scatter.2.cloned.1.call-update
  110.3 0.1 dynamic_slice.40
  110.3 11.9 %reduce-scatter.2.cloned.1.call-done = f32[256,256]{1,0:T(8,128)} async-done(((f32[512,256]{1,0:T(8,128)}), f32[256,256]{1,0:T(8,128)}) %reduce-scatter.2.cloned.1.call-update) | async-done | bytes 262160 | tf_op jit(solution)/shard_map/reduce_scatter | solution.py:86
  122.2 1.1 multiply_reduce_fusion
  123.3 1.1 subtract_divide_fusion
  124.4 8.7 %all_gather.15 = f32[512,256]{1,0:T(8,128)S(1)} all-gather(f32[256,256]{1,0:T(8,128)S(1)} %subtract_divide_fusion), channel_id=1, replica_groups=mesh['dp'=16,'mp'=2] {'mp'}, dimensions={0}, use_global_device_ids=true | all-gather | bytes 786432 | tf_op jit(solution)/shard_map/all_gather | solution.py:92
  133.1 0.8 copy.21
  (57 shorter events, 0.6 us)
Async XLA Ops:
  7.2 47.7 %all-gather.4.cloned.1.call-start = ((), (), s32[]{:S(2)}) async-start(), calls=%async_computation.1 | async-start | bytes 2228224 | tf_op jit(solution)/shard_map/all_gather | solution.py:23
  10.1 112.1 %reduce-scatter.2.cloned.1.call-start = ((), (), s32[]{:S(2)}) async-start(), calls=%async_computation.2 | async-start | bytes 786432 | tf_op jit(solution)/shard_map/reduce_scatter | solution.py:86
  54.9 37.1 %copy-start.1 = (f32[512]{0:T(512)S(1)}, f32[512]{0:T(512)}, u32[]{:S(2)}) copy-start(f32[512]{0:T(512)} %param.9) | copy-start | bytes 6148
  109.4 0.8 copy-start
Sparse Core Ops, SparseCore 0:
  10.7 44.1 all-gather.3
  110.4 11.8 reduce-scatter.1
where the time goes:
time: 141 us
  blocking collectives  55.9 us (40%)
  waiting for transfers between devices  32.7 us (23%)
  matrix products  28.6 us (20%)
  between operations  14.2 us (10%)
  other arithmetic  5.26 us (4%)
  local copies, waits for them, and re-layouts  3.4 us (2%)
    all_gather x1, blocking collectives, shards(): lax.all_gather(weight_mine, 'dp', axis=0, tiled=True)  23.1 us
    all_gather x1, waiting for transfers between devices, shards(): columns = lax.all_gather(mine, 'dp', axis=0, tiled=True)  20.7 us
    all_gather x1, blocking collectives, shards(): lax.all_gather(lse_mine, 'dp', axis=0, tiled=True)  19.2 us
    dot_general x8, matrix products, backward(): jnp.dot(coef, cols_block, preferred_element_type=jnp.float32)  16.8 us
    reduce_scatter x1, waiting for transfers between devices, shards(): lax.psum_scatter(partial_grad, 'mp', scatter_dimension=0, tiled=True)  11.9 us
    dot_general x8, matrix products, tile(): lax.dot_general(normal, cols_block, (((1,), (1,)), ((), ())), preferred_e...  11.8 us
    all_gather x1, blocking collectives, shards(): grad = lax.all_gather(finished, 'mp', axis=0, tiled=True)  8.71 us
    psum x1, blocking collectives, shards(): total, positive = lax.psum((total, positive), 'mp')  4.94 us
  transfers between devices with their start and end apart: 2, of which 2 were waited for; matrix products, arithmetic and copies ran while one was open for 1% of the time, Pallas kernels for 0%

commit v1 on v0

v1 whole, which is shorter than its diff:
```python
import functools
import math

import jax
import jax.numpy as jnp
from jax import lax
from jax.experimental import pallas as pl
from jax.experimental.pallas import tpu as pltpu
from jax.sharding import PartitionSpec as P

INV_TAU = 10.0
EPS = 1e-06
SCALE = INV_TAU / math.log(2.0)
MESH = pl.DeviceIdType.MESH
EXTRA = 16


def fold(x):
    width = x.shape[1]
    if width <= 128:
        return x
    total = x[:, :128]
    for start in range(128, width, 128):
        total = total + x[:, start : start + 128]
    return total


def widen(x, width):
    if width <= 128:
        return x[:, :width]
    return jnp.concatenate([x] * (width // 128), axis=1)


def as_columns(row):
    return jnp.transpose(jnp.broadcast_to(row, (128, row.shape[1])))


def kernel(
    n,
    p,
    views_ref,
    partner_ref,
    weight_ref,
    loss_ref,
    grad_ref,
    rows_bf,
    cols,
    exps,
    scaled,
    acc_u,
    acc_p,
    acc_t,
    acc_w,
    mates,
    stats,
    all_a,
    parts,
    send_z,
    send_y,
    send_c,
    recv_b,
    send_s,
    recv_s,
    send_a,
    recv_a,
    send_g,
    recv_g,
):
    rows, width = views_ref.shape
    piece = rows // p
    chunk = min(128, rows)
    chunks = rows // chunk
    lanes = min(piece, 128)
    depth = n // 4
    me = lax.axis_index("dp")
    slot = lax.axis_index("mp")
    core = lax.rem(me, 2)
    y = lax.rem(lax.div(me, 2), 2)
    z = lax.div(me, 4)

    def place(zz, yy, cc):
        return (zz * 2 + yy) * 2 + cc

    barrier = pltpu.get_barrier_semaphore()

    def greet_dp(k, carry):
        pl.semaphore_signal(
            barrier, inc=1, device_id=(lax.rem(me + k, n), slot), device_id_type=MESH
        )
        return carry

    def greet_mp(k, carry):
        pl.semaphore_signal(
            barrier, inc=1, device_id=(me, lax.rem(slot + k, p)), device_id_type=MESH
        )
        return carry

    lax.fori_loop(1, n, greet_dp, 0)
    lax.fori_loop(1, p, greet_mp, 0)

    def lengths(i):
        at = pl.ds(i * chunk, chunk)
        floats = views_ref[at, :].astype(jnp.float32)
        length = jnp.sqrt(jnp.sum(floats * floats, axis=1, keepdims=True) + EPS)
        return floats, length

    for i in range(chunks):
        floats, length = lengths(i)
        rows_bf[i * chunk : (i + 1) * chunk, :] = (floats / length).astype(jnp.bfloat16)
    start = pl.multiple_of(slot * piece, piece)
    cols[me, 0:piece, :] = rows_bf[pl.ds(start, piece), :]
    weight_row = weight_ref[...]
    high = weight_row.astype(jnp.bfloat16).astype(jnp.float32)
    middle = (weight_row - high).astype(jnp.bfloat16).astype(jnp.float32)
    low = weight_row - high - middle
    terms = jnp.concatenate(
        [high, middle, low, jnp.zeros((EXTRA - 3, rows), jnp.float32)], axis=0
    ).astype(jnp.bfloat16)
    for j in range(p):

        @pl.when(slot == j)
        def _():
            cols[me, piece : piece + EXTRA, 0:piece] = terms[:, j * piece : (j + 1) * piece]

    pl.semaphore_wait(barrier, n + p - 2)

    def block_copy(b, send, device):
        return pltpu.make_async_remote_copy(
            src_ref=cols.at[b],
            dst_ref=cols.at[b],
            send_sem=send,
            recv_sem=recv_b.at[b],
            device_id=(device, slot),
            device_id_type=MESH,
        )

    def up(b):
        return block_copy(b, send_z.at[0, b], place(jnp.minimum(z + 1, depth - 1), y, core))

    def down(b):
        return block_copy(b, send_z.at[1, b], place(jnp.maximum(z - 1, 0), y, core))

    def across(b):
        return block_copy(b, send_y.at[b], place(z, 1 - y, core))

    def sibling(b):
        return block_copy(b, send_c.at[b], place(z, y, 1 - core))

    short = jnp.minimum(z, depth - 1 - z)
    long_below = z > depth - 1 - z

    def line(k):
        paired = k <= 2 * short
        step = jnp.where(paired, lax.div(k + 1, 2), k - short)
        below = jnp.where(paired, lax.rem(k, 2) == 1, long_below)
        return jnp.where(below, z - step, z + step)

    def goes_up(zz):
        return jnp.logical_and(zz <= z, z < depth - 1)

    def goes_down(zz):
        return jnp.logical_and(zz >= z, z > 0)

    def forward(zz, b):
        @pl.when(goes_up(zz))
        def _():
            up(b).start()

        @pl.when(goes_down(zz))
        def _():
            down(b).start()

        across(b).start()
        sibling(b).start()

    forward(z, me)

    acc_u[...] = jnp.zeros_like(acc_u)
    acc_p[...] = jnp.zeros_like(acc_p)
    acc_t[...] = jnp.zeros_like(acc_t)
    acc_w[...] = jnp.zeros_like(acc_w)
    mates[...] = as_columns(partner_ref[...].astype(jnp.float32))

    def compute(b, own):
        block = cols[b, 0:piece, :]
        carried = cols[b, piece : piece + EXTRA, :].astype(jnp.float32)[:, :piece]
        weights = carried[0:1] + carried[1:2] + carried[2:3]
        lane = lax.broadcasted_iota(jnp.int32, (1, piece), 1)
        ids = (lane + (b * rows + slot * piece)).astype(jnp.float32)
        for i in range(chunks):
            at = slice(i * chunk, (i + 1) * chunk)
            s = lax.dot_general(
                rows_bf[at, :],
                block,
                (((1,), (1,)), ((), ())),
                preferred_element_type=jnp.float32,
            )
            e = jnp.exp2(s * SCALE)
            if own:
                here = lax.broadcasted_iota(jnp.int32, (chunk, piece), 0) + i * chunk
                there = lax.broadcasted_iota(jnp.int32, (chunk, piece), 1) + slot * piece
                e = jnp.where(here == there, 0.0, e)
            acc_t[at, :] += fold(e)
            match = widen(mates[at, :], piece) == ids
            acc_w[at, :] += fold(jnp.where(match, weights, 0.0))
            hit = jnp.where(match, 1.0, 0.0).astype(jnp.bfloat16)
            rounded = e.astype(jnp.bfloat16)
            exps[b, at, :] = rounded
            acc_u[at, :] += jnp.dot(rounded, block, preferred_element_type=jnp.float32)
            acc_p[at, :] += jnp.dot(hit, block, preferred_element_type=jnp.float32)

    compute(me, True)

    def arrived(b):
        sibling(b).wait_recv()

    def late(k):
        zz = line(k)
        b = place(zz, 1 - y, core)
        arrived(b)
        sibling(b).start()

        def one(j, carry):
            yy = jnp.where(j == 1, y, 1 - y)
            cc = jnp.where(j == 0, core, 1 - core)
            b = place(zz, yy, cc)

            @pl.when(j > 0)
            def _():
                arrived(b)

            compute(b, False)
            return carry

        lax.fori_loop(0, 3, one, 0)

    def body(k, carry):
        @pl.when(k < depth)
        def _():
            zz = line(k)
            b = place(zz, y, core)
            arrived(b)
            forward(zz, b)
            compute(b, False)

        late(k - 1)
        return carry

    lax.fori_loop(1, depth + 1, body, 0)

    positive = []
    for i in range(chunks):
        at = slice(i * chunk, (i + 1) * chunk)
        positive.append(fold(rows_bf[at, :].astype(jnp.float32) * acc_p[at, :]))
    positive = jnp.concatenate(positive, axis=0)
    total_row = jnp.sum(jnp.transpose(acc_t[...]), axis=0, keepdims=True)
    positive_row = INV_TAU * jnp.sum(jnp.transpose(positive), axis=0, keepdims=True)
    stats[slot] = jnp.concatenate(
        [total_row, positive_row, jnp.zeros((6, rows), jnp.float32)], axis=0
    )

    def stats_copy(source, k):
        return pltpu.make_async_remote_copy(
            src_ref=stats.at[source],
            dst_ref=stats.at[source],
            send_sem=send_s.at[k],
            recv_sem=recv_s.at[source],
            device_id=(me, lax.rem(slot + k, p)),
            device_id_type=MESH,
        )

    for k in range(1, p):
        stats_copy(slot, k).start()
    for k in range(1, p):
        stats_copy(lax.rem(slot + k, p), k).wait_recv()
    both = stats[0]
    for j in range(1, p):
        both = both + stats[j]
    total_row = both[0:1]
    loss_ref[...] = jnp.log(total_row) - both[1:2]
    share_row = weight_row / total_row
    for j in range(p):

        @pl.when(slot == j)
        def _():
            all_a[me] = share_row[:, j * piece : (j + 1) * piece]

    def a_copy(source, k):
        return pltpu.make_async_remote_copy(
            src_ref=all_a.at[source],
            dst_ref=all_a.at[source],
            send_sem=send_a.at[k],
            recv_sem=recv_a.at[source],
            device_id=(lax.rem(me + k, n), slot),
            device_id_type=MESH,
        )

    def send_all(k, carry):
        a_copy(me, k).start()
        return carry

    lax.fori_loop(1, n, send_all, 0)

    share_col = as_columns(share_row)
    weight_col = as_columns(weight_row)
    for i in range(chunks):
        at = slice(i * chunk, (i + 1) * chunk)
        mate = jnp.sum(acc_w[at, :], axis=1, keepdims=True)
        acc_u[at, :] = (
            widen(share_col[at, :], width) * acc_u[at, :]
            - (widen(weight_col[at, :], width) + mate) * acc_p[at, :]
        )

    def scale(k, carry):
        d = lax.rem(me + k, n)

        @pl.when(k > 0)
        def _():
            a_copy(d, k).wait_recv()

        factor = widen(as_columns(all_a[d]), width)
        scaled[d] = (cols[d, 0:piece, :].astype(jnp.float32) * factor).astype(jnp.bfloat16)
        return carry

    lax.fori_loop(0, n, scale, 0)

    def g_copy(source, i, k):
        at = pl.ds(i * chunk, chunk)
        return pltpu.make_async_remote_copy(
            src_ref=parts.at[source, at],
            dst_ref=parts.at[source, at],
            send_sem=send_g.at[k, i],
            recv_sem=recv_g.at[source, i],
            device_id=(me, lax.rem(slot + k, p)),
            device_id_type=MESH,
        )

    for i in range(chunks):
        at = slice(i * chunk, (i + 1) * chunk)
        g = acc_u[at, :]
        for d in range(n):
            g = g + jnp.dot(exps[d, at, :], scaled[d], preferred_element_type=jnp.float32)
        g = g * INV_TAU
        floats, length = lengths(i)
        unit = floats / length
        along = jnp.sum(unit * g, axis=1, keepdims=True)
        parts[slot, at, :] = ((g - unit * along) / length).astype(jnp.bfloat16)
        for k in range(1, p):
            g_copy(slot, i, k).start()
    for i in range(chunks):
        at = slice(i * chunk, (i + 1) * chunk)
        for k in range(1, p):
            g_copy(lax.rem(slot + k, p), i, k).wait_recv()
        total = parts[0, at, :].astype(jnp.float32)
        for j in range(1, p):
            total = total + parts[j, at, :].astype(jnp.float32)
        grad_ref[at, :] = total

    def drain(k, carry):
        zz = line(k)
        b = place(zz, y, core)

        @pl.when(goes_up(zz))
        def _():
            up(b).wait_send()

        @pl.when(goes_down(zz))
        def _():
            down(b).wait_send()

        across(b).wait_send()
        sibling(b).wait_send()
        sibling(place(zz, 1 - y, core)).wait_send()
        return carry

    lax.fori_loop(0, depth, drain, 0)

    def drain_a(k, carry):
        a_copy(me, k).wait_send()
        return carry

    lax.fori_loop(1, n, drain_a, 0)
    for k in range(1, p):
        stats_copy(slot, k).wait_send()
        for i in range(chunks):
            g_copy(slot, i, k).wait_send()


def shards(n, p, views, partner, weight):
    rows, width = views.shape
    piece = rows // p
    lanes = min(piece, 128)
    chunks = rows // min(128, rows)
    dma = pltpu.SemaphoreType.DMA
    vmem = pl.BlockSpec(memory_space=pltpu.VMEM)
    loss, grad = pl.pallas_call(
        functools.partial(kernel, n, p),
        out_shape=(
            jax.ShapeDtypeStruct((1, rows), jnp.float32),
            jax.ShapeDtypeStruct((rows, width), jnp.float32),
        ),
        in_specs=[vmem] * 3,
        out_specs=(vmem, vmem),
        scratch_shapes=[
            pltpu.VMEM((rows, width), jnp.bfloat16),
            pltpu.VMEM((n, piece + EXTRA, width), jnp.bfloat16),
            pltpu.VMEM((n, rows, piece), jnp.bfloat16),
            pltpu.VMEM((n, piece, width), jnp.bfloat16),
            pltpu.VMEM((rows, width), jnp.float32),
            pltpu.VMEM((rows, width), jnp.float32),
            pltpu.VMEM((rows, lanes), jnp.float32),
            pltpu.VMEM((rows, lanes), jnp.float32),
            pltpu.VMEM((rows, 128), jnp.float32),
            pltpu.VMEM((p, 8, rows), jnp.float32),
            pltpu.VMEM((n, 1, piece), jnp.float32),
            pltpu.VMEM((p, rows, width), jnp.bfloat16),
            dma((2, n)),
            dma((n,)),
            dma((n,)),
            dma((n,)),
            dma((p,)),
            dma((p,)),
            dma((n,)),
            dma((n,)),
            dma((p, chunks)),
            dma((p, chunks)),
        ],
        compiler_params=pltpu.CompilerParams(
            collective_id=0, has_side_effects=True, vmem_limit_bytes=40 * 1024 * 1024
        ),
    )(views, partner.reshape(1, rows), weight.reshape(1, rows))
    return loss.reshape(rows), grad


def solution(mesh):
    n, p = mesh.shape["dp"], mesh.shape["mp"]
    return jax.shard_map(
        functools.partial(shards, n, p),
        mesh=mesh,
        in_specs=(P("dp", None), P("dp"), P("dp")),
        out_specs=(P("dp"), P("dp", None)),
        check_vma=False,
    )
```

time: 141 us -> 50 us (0.35)
  blocking collectives: 55.9 us -> 0 us
  Pallas kernels: 0 us -> 45.4 us
  waiting for transfers between devices: 32.7 us -> 0 us
  matrix products: 28.6 us -> 0 us
  between operations: 14.2 us -> 0.65 us
  other arithmetic: 5.26 us -> 0 us
    all_gather x3 -> x0, blocking collectives: 51 us -> none  [the longest x1 23.1 us: shards(): lax.all_gather(weight_mine, 'dp', axis=0, tiled=True)]
    pallas_call x0 -> x1, Pallas kernels: none -> 45.4 us  [shards(): pl.pallas_call(functools.partial(kernel, n, p), out_shape=(jax.ShapeDtype...]
    dot_general x16 -> x0, matrix products: 28.6 us -> none  [the longest x8 16.8 us: backward(): jnp.dot(coef, cols_block, preferred_element_type=jnp.float32)]
    all_gather x1 -> x0, waiting for transfers between devices: 20.7 us -> none  [shards(): columns = lax.all_gather(mine, 'dp', axis=0, tiled=True)]
    reduce_scatter x1 -> x0, waiting for transfers between devices: 11.9 us -> none  [shards(): lax.psum_scatter(partial_grad, 'mp', scatter_dimension=0, tiled=True)]
    psum x1 -> x0, blocking collectives: 4.94 us -> none  [shards(): total, positive = lax.psum((total, positive), 'mp')]
    div x2 -> x0, other arithmetic: 2.18 us -> none  [the longest x1 1.09 us: shards(): unit = floats / length[:, None]]
    reduce_sum x2 -> x0, other arithmetic: 2.16 us -> none  [the longest x1 1.1 us: shards(): length = jnp.sqrt(jnp.sum(floats * floats, axis=1) + EPS)]
  transfers between devices with their start and end apart: 2 -> 0, of which waited for: 2 -> 0; matrix products, arithmetic and copies ran while one was open for 1% -> 0% of each run, Pallas kernels for 0% -> 0%
where the time goes in v1:
time: 50 us; the launch traced here: 49.8 us
  Pallas kernels  45.4 us (91%)
  local copies, waits for them, and re-layouts  3.68 us (7%)
  between operations  0.65 us (1%)
    pallas_call x1, Pallas kernels, shards(): pl.pallas_call(functools.partial(kernel, n, p), out_shape=(jax.ShapeDtype...  45.4 us
    unnamed x8, local copies, waits for them, and re-layouts  3.68 us

profile of v1, /device:TPU:0, one launch (start us, length us, event | category | flops | bytes accessed | tf_op | source)
XLA Modules:
  0.0 49.8 jit_solution(4825180445961420293)
XLA Ops:
  0.6 0.0 copy-start.1
  0.6 0.7 %copy-done.1 = s32[512]{0:T(512)S(1)} copy-done((s32[512]{0:T(512)S(1)}, s32[512]{0:T(512)}, u32[]{:S(2)}) %copy-start.1) | copy-done | bytes 2072
  1.3 0.0 copy-start
  1.3 0.9 %copy-done = bf16[512,256]{1,0:T(8,128)(2,1)S(1)} copy-done((bf16[512,256]{1,0:T(8,128)(2,1)S(1)}, bf16[512,256]{1,0:T(8,128)(2,1)}, u32[]{:S(2)}) %copy-start) | copy-done | bytes 262168
  2.3 0.0 copy-start.2
  2.3 0.7 %copy-done.2 = f32[512]{0:T(512)S(1)} copy-done((f32[512]{0:T(512)S(1)}, f32[512]{0:T(512)}, u32[]{:S(2)}) %copy-start.2) | copy-done | bytes 2072
  2.9 45.4 %shard_map.50 = (f32[1,512]{1,0:T(1,128)S(1)}, f32[512,256]{1,0:T(8,128)S(1)}) custom-call(bf16[512,256]{1,0:T(8,128)(2,1)S(1)} %copy-done, s32[1,512]{1,0:T(1,128)S(1)} %bitcast.3, f32[1,512]{1,0:T(1,128)S(1)} %bitcast.4), custom_call_target="tpu_custom_call" | custom-call | tf_op jit(solution)/shard_map/pallas_call | solution.py:396
  48.4 0.6 %copy.7 = f32[512]{0:T(512)} copy(f32[512]{0:T(512)S(1)} %bitcast.5) | data formatting | bytes 4096
  49.0 0.8 %copy.8 = f32[512,256]{1,0:T(8,128)} copy(f32[512,256]{1,0:T(8,128)S(1)} %get-tuple-element.9) | data formatting | bytes 1048576
Async XLA Ops:
  0.6 0.7 %copy-start.1 = (s32[512]{0:T(512)S(1)}, s32[512]{0:T(512)}, u32[]{:S(2)}) copy-start(s32[512]{0:T(512)} %param.4) | copy-start | bytes 6148
  1.3 0.9 %copy-start = (bf16[512,256]{1,0:T(8,128)(2,1)S(1)}, bf16[512,256]{1,0:T(8,128)(2,1)}, u32[]{:S(2)}) copy-start(bf16[512,256]{1,0:T(8,128)(2,1)} %views_ref.1) | copy-start | bytes 786436
  2.3 0.7 %copy-start.2 = (f32[512]{0:T(512)S(1)}, f32[512]{0:T(512)}, u32[]{:S(2)}) copy-start(f32[512]{0:T(512)} %param.5) | copy-start | bytes 6148

commit v2 on v1

--- a/solution.py
+++ b/solution.py
@@ -12,6 +12,7 @@
 EPS = 1e-06
 SCALE = INV_TAU / math.log(2.0)
 MESH = pl.DeviceIdType.MESH
+SUBS = 4
 EXTRA = 16
 
 
@@ -83,11 +84,19 @@
 
     barrier = pltpu.get_barrier_semaphore()
 
-    def greet_dp(k, carry):
-        pl.semaphore_signal(
-            barrier, inc=1, device_id=(lax.rem(me + k, n), slot), device_id_type=MESH
-        )
-        return carry
+    def greet(device):
+        pl.semaphore_signal(barrier, inc=1, device_id=(device, slot), device_id_type=MESH)
+
+    greet(place(z, y, 1 - core))
+    greet(place(z, 1 - y, core))
+
+    @pl.when(z < depth - 1)
+    def _():
+        greet(place(z + 1, y, core))
+
+    @pl.when(z > 0)
+    def _():
+        greet(place(z - 1, y, core))
 
     def greet_mp(k, carry):
         pl.semaphore_signal(
@@ -95,20 +104,19 @@
         )
         return carry
 
-    lax.fori_loop(1, n, greet_dp, 0)
     lax.fori_loop(1, p, greet_mp, 0)
 
-    def lengths(i):
-        at = pl.ds(i * chunk, chunk)
-        floats = views_ref[at, :].astype(jnp.float32)
+    def lengths(start, count):
+        floats = views_ref[pl.ds(start, count), :].astype(jnp.float32)
         length = jnp.sqrt(jnp.sum(floats * floats, axis=1, keepdims=True) + EPS)
         return floats, length
 
-    for i in range(chunks):
-        floats, length = lengths(i)
-        rows_bf[i * chunk : (i + 1) * chunk, :] = (floats / length).astype(jnp.bfloat16)
-    start = pl.multiple_of(slot * piece, piece)
-    cols[me, 0:piece, :] = rows_bf[pl.ds(start, piece), :]
+    part = min(chunk, piece)
+    for i in range(piece // part):
+        start = pl.multiple_of(slot * piece + i * part, part)
+        floats, length = lengths(start, part)
+        at = slice(EXTRA + i * part, EXTRA + (i + 1) * part)
+        cols[me, at, :] = (floats / length).astype(jnp.bfloat16)
     weight_row = weight_ref[...]
     high = weight_row.astype(jnp.bfloat16).astype(jnp.float32)
     middle = (weight_row - high).astype(jnp.bfloat16).astype(jnp.float32)
@@ -120,31 +128,35 @@
 
         @pl.when(slot == j)
         def _():
-            cols[me, piece : piece + EXTRA, 0:piece] = terms[:, j * piece : (j + 1) * piece]
-
-    pl.semaphore_wait(barrier, n + p - 2)
-
-    def block_copy(b, send, device):
+            cols[me, 0:EXTRA, 0:piece] = terms[:, j * piece : (j + 1) * piece]
+
+    ends = jnp.where(z == 0, 1, 0) + jnp.where(z == depth - 1, 1, 0)
+    pl.semaphore_wait(barrier, 4 + p - 1 - ends)
+
+    sub = piece // SUBS
+
+    def block_copy(b, j, send, device):
+        at = pl.ds(0, EXTRA + sub) if j == 0 else pl.ds(EXTRA + j * sub, sub)
         return pltpu.make_async_remote_copy(
-            src_ref=cols.at[b],
-            dst_ref=cols.at[b],
+            src_ref=cols.at[b, at],
+            dst_ref=cols.at[b, at],
             send_sem=send,
-            recv_sem=recv_b.at[b],
+            recv_sem=recv_b.at[b, j],
             device_id=(device, slot),
             device_id_type=MESH,
         )
 
-    def up(b):
-        return block_copy(b, send_z.at[0, b], place(jnp.minimum(z + 1, depth - 1), y, core))
-
-    def down(b):
-        return block_copy(b, send_z.at[1, b], place(jnp.maximum(z - 1, 0), y, core))
-
-    def across(b):
-        return block_copy(b, send_y.at[b], place(z, 1 - y, core))
-
-    def sibling(b):
-        return block_copy(b, send_c.at[b], place(z, y, 1 - core))
+    def up(b, j):
+        return block_copy(b, j, send_z.at[0, b, j], place(jnp.minimum(z + 1, depth - 1), y, core))
+
+    def down(b, j):
+        return block_copy(b, j, send_z.at[1, b, j], place(jnp.maximum(z - 1, 0), y, core))
+
+    def across(b, j):
+        return block_copy(b, j, send_y.at[b, j], place(z, 1 - y, core))
+
+    def sibling(b, j):
+        return block_copy(b, j, send_c.at[b, j], place(z, y, 1 - core))
 
     short = jnp.minimum(z, depth - 1 - z)
     long_below = z > depth - 1 - z
@@ -161,20 +173,24 @@
     def goes_down(zz):
         return jnp.logical_and(zz >= z, z > 0)
 
-    def forward(zz, b):
+    def forward(zz, b, j):
         @pl.when(goes_up(zz))
         def _():
-            up(b).start()
+            up(b, j).start()
 
         @pl.when(goes_down(zz))
         def _():
-            down(b).start()
-
-        across(b).start()
-        sibling(b).start()
-
-    forward(z, me)
-
+            down(b, j).start()
+
+        across(b, j).start()
+        sibling(b, j).start()
+
+    for j in range(SUBS):
+        forward(z, me, j)
+
+    for i in range(chunks):
+        floats, length = lengths(i * chunk, chunk)
+        rows_bf[i * chunk : (i + 1) * chunk, :] = (floats / length).astype(jnp.bfloat16)
     acc_u[...] = jnp.zeros_like(acc_u)
     acc_p[...] = jnp.zeros_like(acc_p)
     acc_t[...] = jnp.zeros_like(acc_t)
@@ -182,8 +198,8 @@
     mates[...] = as_columns(partner_ref[...].astype(jnp.float32))
 
     def compute(b, own):
-        block = cols[b, 0:piece, :]
-        carried = cols[b, piece : piece + EXTRA, :].astype(jnp.float32)[:, :piece]
+        block = cols[b, EXTRA : EXTRA + piece, :]
+        carried = cols[b, 0:EXTRA, :].astype(jnp.float32)[:, :piece]
         weights = carried[0:1] + carried[1:2] + carried[2:3]
         lane = lax.broadcasted_iota(jnp.int32, (1, piece), 1)
         ids = (lane + (b * rows + slot * piece)).astype(jnp.float32)
@@ -209,44 +225,64 @@
             acc_u[at, :] += jnp.dot(rounded, block, preferred_element_type=jnp.float32)
             acc_p[at, :] += jnp.dot(hit, block, preferred_element_type=jnp.float32)
 
-    compute(me, True)
-
-    def arrived(b):
-        sibling(b).wait_recv()
-
-    def late(k):
-        zz = line(k)
-        b = place(zz, 1 - y, core)
-        arrived(b)
-        sibling(b).start()
-
-        def one(j, carry):
-            yy = jnp.where(j == 1, y, 1 - y)
-            cc = jnp.where(j == 0, core, 1 - core)
-            b = place(zz, yy, cc)
-
-            @pl.when(j > 0)
+    def arrived(b, j):
+        sibling(b, j).wait_recv()
+
+    def body(t, carry):
+        ahead = line(t + 1)
+        now = line(t)
+        before = line(t - 1)
+        for j in range(SUBS):
+
+            @pl.when(t < depth - 1)
             def _():
-                arrived(b)
-
-            compute(b, False)
-            return carry
-
-        lax.fori_loop(0, 3, one, 0)
-
-    def body(k, carry):
-        @pl.when(k < depth)
-        def _():
-            zz = line(k)
-            b = place(zz, y, core)
-            arrived(b)
-            forward(zz, b)
-            compute(b, False)
-
-        late(k - 1)
-        return carry
-
-    lax.fori_loop(1, depth + 1, body, 0)
+                b = place(ahead, y, core)
+                arrived(b, j)
+                forward(ahead, b, j)
+
+            @pl.when(t < depth)
+            def _():
+                b = place(now, 1 - y, core)
+                arrived(b, j)
+                sibling(b, j).start()
+
+            if j == 0:
+
+                @pl.when(t == 0)
+                def _():
+                    compute(me, True)
+
+                @pl.when(jnp.logical_and(t > 0, t < depth))
+                def _():
+                    compute(place(now, y, core), False)
+
+            if j == 1:
+
+                @pl.when(t > 0)
+                def _():
+                    compute(place(before, 1 - y, core), False)
+
+            if j == 2:
+
+                @pl.when(t < depth)
+                def _():
+                    b = place(now, y, 1 - core)
+                    for q in range(SUBS):
+                        arrived(b, q)
+                    compute(b, False)
+
+            if j == 3:
+
+                @pl.when(t > 0)
+                def _():
+                    b = place(before, 1 - y, 1 - core)
+                    for q in range(SUBS):
+                        arrived(b, q)
+                    compute(b, False)
+
+        return carry
+
+    lax.fori_loop(0, depth + 1, body, 0)
 
     positive = []
     for i in range(chunks):
@@ -256,7 +292,7 @@
     total_row = jnp.sum(jnp.transpose(acc_t[...]), axis=0, keepdims=True)
     positive_row = INV_TAU * jnp.sum(jnp.transpose(positive), axis=0, keepdims=True)
     stats[slot] = jnp.concatenate(
-        [total_row, positive_row, jnp.zeros((6, rows), jnp.float32)], axis=0
+        [total_row, positive_row], axis=0
     )
 
     def stats_copy(source, k):
@@ -319,7 +355,7 @@
             a_copy(d, k).wait_recv()
 
         factor = widen(as_columns(all_a[d]), width)
-        scaled[d] = (cols[d, 0:piece, :].astype(jnp.float32) * factor).astype(jnp.bfloat16)
+        scaled[d] = (cols[d, EXTRA : EXTRA + piece, :].astype(jnp.float32) * factor).astype(jnp.bfloat16)
         return carry
 
     lax.fori_loop(0, n, scale, 0)
@@ -341,12 +377,41 @@
         for d in range(n):
             g = g + jnp.dot(exps[d, at, :], scaled[d], preferred_element_type=jnp.float32)
         g = g * INV_TAU
-        floats, length = lengths(i)
+        floats, length = lengths(i * chunk, chunk)
         unit = floats / length
         along = jnp.sum(unit * g, axis=1, keepdims=True)
         parts[slot, at, :] = ((g - unit * along) / length).astype(jnp.bfloat16)
         for k in range(1, p):
             g_copy(slot, i, k).start()
+    def drain(k, carry):
+        zz = line(k)
+        b = place(zz, y, core)
+        other = place(zz, 1 - y, core)
+        for j in range(SUBS):
+
+            @pl.when(goes_up(zz))
+            def _():
+                up(b, j).wait_send()
+
+            @pl.when(goes_down(zz))
+            def _():
+                down(b, j).wait_send()
+
+            across(b, j).wait_send()
+            sibling(b, j).wait_send()
+            sibling(other, j).wait_send()
+        return carry
+
+    lax.fori_loop(0, depth, drain, 0)
+
+    def drain_a(k, carry):
+        a_copy(me, k).wait_send()
+        return carry
+
+    lax.fori_loop(1, n, drain_a, 0)
+    for k in range(1, p):
+        stats_copy(slot, k).wait_send()
+
     for i in range(chunks):
         at = slice(i * chunk, (i + 1) * chunk)
         for k in range(1, p):
@@ -355,33 +420,7 @@
         for j in range(1, p):
             total = total + parts[j, at, :].astype(jnp.float32)
         grad_ref[at, :] = total
-
-    def drain(k, carry):
-        zz = line(k)
-        b = place(zz, y, core)
-
-        @pl.when(goes_up(zz))
-        def _():
-            up(b).wait_send()
-
-        @pl.when(goes_down(zz))
-        def _():
-            down(b).wait_send()
-
-        across(b).wait_send()
-        sibling(b).wait_send()
-        sibling(place(zz, 1 - y, core)).wait_send()
-        return carry
-
-    lax.fori_loop(0, depth, drain, 0)
-
-    def drain_a(k, carry):
-        a_copy(me, k).wait_send()
-        return carry
-
-    lax.fori_loop(1, n, drain_a, 0)
     for k in range(1, p):
-        stats_copy(slot, k).wait_send()
         for i in range(chunks):
             g_copy(slot, i, k).wait_send()
 
@@ -411,13 +450,13 @@
             pltpu.VMEM((rows, lanes), jnp.float32),
             pltpu.VMEM((rows, lanes), jnp.float32),
             pltpu.VMEM((rows, 128), jnp.float32),
-            pltpu.VMEM((p, 8, rows), jnp.float32),
+            pltpu.VMEM((p, 2, rows), jnp.float32),
             pltpu.VMEM((n, 1, piece), jnp.float32),
             pltpu.VMEM((p, rows, width), jnp.bfloat16),
-            dma((2, n)),
-            dma((n,)),
-            dma((n,)),
-            dma((n,)),
+            dma((2, n, SUBS)),
+            dma((n, SUBS)),
+            dma((n, SUBS)),
+            dma((n, SUBS)),
             dma((p,)),
             dma((p,)),
             dma((n,)),
@@ -426,7 +465,7 @@
             dma((p, chunks)),
         ],
         compiler_params=pltpu.CompilerParams(
-            collective_id=0, has_side_effects=True, vmem_limit_bytes=40 * 1024 * 1024
+            collective_id=0, has_side_effects=True, vmem_limit_bytes=48 * 1024 * 1024
         ),
     )(views, partner.reshape(1, rows), weight.reshape(1, rows))
     return loss.reshape(rows), grad

time: 50 us -> 47.4 us (0.948)
  Pallas kernels: 45.4 us -> 42.9 us
    pallas_call x1, Pallas kernels: 45.4 us -> 42.9 us  [shards(): pl.pallas_call(functools.partial(kernel, n, p), out_shape=(jax.ShapeDtype...]
where the time goes in v2:
time: 47.4 us; the launch traced here: 47.2 us
  Pallas kernels  42.9 us (91%)
  local copies, waits for them, and re-layouts  3.68 us (8%)
  between operations  0.65 us (1%)
    pallas_call x1, Pallas kernels, shards(): pl.pallas_call(functools.partial(kernel, n, p), out_shape=(jax.ShapeDtype...  42.9 us
    unnamed x8, local copies, waits for them, and re-layouts  3.68 us

profile of v2, /device:TPU:0, one launch (start us, length us, event | category | flops | bytes accessed | tf_op | source)
XLA Modules:
  0.0 47.2 jit_solution(4517551403039123089)
XLA Ops:
  0.6 0.0 copy-start.1
  0.6 0.7 %copy-done.1 = s32[512]{0:T(512)S(1)} copy-done((s32[512]{0:T(512)S(1)}, s32[512]{0:T(512)}, u32[]{:S(2)}) %copy-start.1) | copy-done | bytes 2072
  1.3 0.0 copy-start
  1.3 0.9 %copy-done = bf16[512,256]{1,0:T(8,128)(2,1)S(1)} copy-done((bf16[512,256]{1,0:T(8,128)(2,1)S(1)}, bf16[512,256]{1,0:T(8,128)(2,1)}, u32[]{:S(2)}) %copy-start) | copy-done | bytes 262168
  2.3 0.0 copy-start.2
  2.3 0.7 %copy-done.2 = f32[512]{0:T(512)S(1)} copy-done((f32[512]{0:T(512)S(1)}, f32[512]{0:T(512)}, u32[]{:S(2)}) %copy-start.2) | copy-done | bytes 2072
  2.9 42.9 %shard_map.50 = (f32[1,512]{1,0:T(1,128)S(1)}, f32[512,256]{1,0:T(8,128)S(1)}) custom-call(bf16[512,256]{1,0:T(8,128)(2,1)S(1)} %copy-done, s32[1,512]{1,0:T(1,128)S(1)} %bitcast.3, f32[1,512]{1,0:T(1,128)S(1)} %bitcast.4), custom_call_target="tpu_custom_call" | custom-call | tf_op jit(solution)/shard_map/pallas_call | solution.py:435
  45.8 0.6 %copy.7 = f32[512]{0:T(512)} copy(f32[512]{0:T(512)S(1)} %bitcast.5) | data formatting | bytes 4096
  46.4 0.8 %copy.8 = f32[512,256]{1,0:T(8,128)} copy(f32[512,256]{1,0:T(8,128)S(1)} %get-tuple-element.9) | data formatting | bytes 1048576
Async XLA Ops:
  0.6 0.7 %copy-start.1 = (s32[512]{0:T(512)S(1)}, s32[512]{0:T(512)}, u32[]{:S(2)}) copy-start(s32[512]{0:T(512)} %param.4) | copy-start | bytes 6148
  1.3 0.9 %copy-start = (bf16[512,256]{1,0:T(8,128)(2,1)S(1)}, bf16[512,256]{1,0:T(8,128)(2,1)}, u32[]{:S(2)}) copy-start(bf16[512,256]{1,0:T(8,128)(2,1)} %views_ref.1) | copy-start | bytes 786436
  2.3 0.7 %copy-start.2 = (f32[512]{0:T(512)S(1)}, f32[512]{0:T(512)}, u32[]{:S(2)}) copy-start(f32[512]{0:T(512)} %param.5) | copy-start | bytes 6148

commit v3 on v2

--- a/solution.py
+++ b/solution.py
@@ -174,6 +174,8 @@
         return jnp.logical_and(zz >= z, z > 0)
 
     def forward(zz, b, j):
+        across(b, j).start()
+
         @pl.when(goes_up(zz))
         def _():
             up(b, j).start()
@@ -182,7 +184,6 @@
         def _():
             down(b, j).start()
 
-        across(b, j).start()
         sibling(b, j).start()
 
     for j in range(SUBS):
@@ -284,36 +285,41 @@
 
     lax.fori_loop(0, depth + 1, body, 0)
 
+    def stats_copy(what, source, k):
+        return pltpu.make_async_remote_copy(
+            src_ref=stats.at[what, source],
+            dst_ref=stats.at[what, source],
+            send_sem=send_s.at[what, k],
+            recv_sem=recv_s.at[what, source],
+            device_id=(me, lax.rem(slot + k, p)),
+            device_id_type=MESH,
+        )
+
+    def stats_sum(what):
+        for k in range(1, p):
+            stats_copy(what, lax.rem(slot + k, p), k).wait_recv()
+        result = stats[what, 0]
+        for j in range(1, p):
+            result = result + stats[what, j]
+        return result
+
+    stats[0, slot] = jnp.sum(jnp.transpose(acc_t[...]), axis=0, keepdims=True)
+    for k in range(1, p):
+        stats_copy(0, slot, k).start()
     positive = []
     for i in range(chunks):
         at = slice(i * chunk, (i + 1) * chunk)
         positive.append(fold(rows_bf[at, :].astype(jnp.float32) * acc_p[at, :]))
     positive = jnp.concatenate(positive, axis=0)
-    total_row = jnp.sum(jnp.transpose(acc_t[...]), axis=0, keepdims=True)
-    positive_row = INV_TAU * jnp.sum(jnp.transpose(positive), axis=0, keepdims=True)
-    stats[slot] = jnp.concatenate(
-        [total_row, positive_row], axis=0
-    )
-
-    def stats_copy(source, k):
-        return pltpu.make_async_remote_copy(
-            src_ref=stats.at[source],
-            dst_ref=stats.at[source],
-            send_sem=send_s.at[k],
-            recv_sem=recv_s.at[source],
-            device_id=(me, lax.rem(slot + k, p)),
-            device_id_type=MESH,
-        )
-
+    stats[1, slot] = INV_TAU * jnp.sum(jnp.transpose(positive), axis=0, keepdims=True)
     for k in range(1, p):
-        stats_copy(slot, k).start()
-    for k in range(1, p):
-        stats_copy(lax.rem(slot + k, p), k).wait_recv()
-    both = stats[0]
-    for j in range(1, p):
-        both = both + stats[j]
-    total_row = both[0:1]
-    loss_ref[...] = jnp.log(total_row) - both[1:2]
+        stats_copy(1, slot, k).start()
+    weight_col = as_columns(weight_row)
+    for i in range(chunks):
+        at = slice(i * chunk, (i + 1) * chunk)
+        mate = jnp.sum(acc_w[at, :], axis=1, keepdims=True)
+        acc_p[at, :] = (widen(weight_col[at, :], width) + mate) * acc_p[at, :]
+    total_row = stats_sum(0)
     share_row = weight_row / total_row
     for j in range(p):
 
@@ -338,13 +344,12 @@
     lax.fori_loop(1, n, send_all, 0)
 
     share_col = as_columns(share_row)
-    weight_col = as_columns(weight_row)
+    loss_ref[...] = jnp.log(total_row) - stats_sum(1)
     for i in range(chunks):
         at = slice(i * chunk, (i + 1) * chunk)
-        mate = jnp.sum(acc_w[at, :], axis=1, keepdims=True)
         acc_u[at, :] = (
             widen(share_col[at, :], width) * acc_u[at, :]
-            - (widen(weight_col[at, :], width) + mate) * acc_p[at, :]
+            - acc_p[at, :]
         )
 
     def scale(k, carry):
@@ -410,7 +415,8 @@
 
     lax.fori_loop(1, n, drain_a, 0)
     for k in range(1, p):
-        stats_copy(slot, k).wait_send()
+        stats_copy(0, slot, k).wait_send()
+        stats_copy(1, slot, k).wait_send()
 
     for i in range(chunks):
         at = slice(i * chunk, (i + 1) * chunk)
@@ -450,15 +456,15 @@
             pltpu.VMEM((rows, lanes), jnp.float32),
             pltpu.VMEM((rows, lanes), jnp.float32),
             pltpu.VMEM((rows, 128), jnp.float32),
-            pltpu.VMEM((p, 2, rows), jnp.float32),
+            pltpu.VMEM((2, p, 1, rows), jnp.float32),
             pltpu.VMEM((n, 1, piece), jnp.float32),
             pltpu.VMEM((p, rows, width), jnp.bfloat16),
             dma((2, n, SUBS)),
             dma((n, SUBS)),
             dma((n, SUBS)),
             dma((n, SUBS)),
-            dma((p,)),
-            dma((p,)),
+            dma((2, p)),
+            dma((2, p)),
             dma((n,)),
             dma((n,)),
             dma((p, chunks)),

time: 47.4 us -> 47.4 us (level)
  no operation moved by 1% of the time
where the time goes in v3:
time: 47.4 us; the launch traced here: 47.2 us
  Pallas kernels  42.8 us (90%)
  local copies, waits for them, and re-layouts  3.68 us (8%)
  between operations  0.65 us (1%)
    pallas_call x1, Pallas kernels, shards(): pl.pallas_call(functools.partial(kernel, n, p), out_shape=(jax.ShapeDtype...  42.8 us
    unnamed x8, local copies, waits for them, and re-layouts  3.68 us

profile of v3, /device:TPU:0, one launch (start us, length us, event | category | flops | bytes accessed | tf_op | source)
XLA Modules:
  0.0 47.2 jit_solution(5633294036986556505)
XLA Ops:
  0.6 0.0 copy-start.1
  0.6 0.7 %copy-done.1 = s32[512]{0:T(512)S(1)} copy-done((s32[512]{0:T(512)S(1)}, s32[512]{0:T(512)}, u32[]{:S(2)}) %copy-start.1) | copy-done | bytes 2072
  1.3 0.0 copy-start
  1.3 0.9 %copy-done = bf16[512,256]{1,0:T(8,128)(2,1)S(1)} copy-done((bf16[512,256]{1,0:T(8,128)(2,1)S(1)}, bf16[512,256]{1,0:T(8,128)(2,1)}, u32[]{:S(2)}) %copy-start) | copy-done | bytes 262168
  2.3 0.0 copy-start.2
  2.3 0.7 %copy-done.2 = f32[512]{0:T(512)S(1)} copy-done((f32[512]{0:T(512)S(1)}, f32[512]{0:T(512)}, u32[]{:S(2)}) %copy-start.2) | copy-done | bytes 2072
  2.9 42.8 %shard_map.50 = (f32[1,512]{1,0:T(1,128)S(1)}, f32[512,256]{1,0:T(8,128)S(1)}) custom-call(bf16[512,256]{1,0:T(8,128)(2,1)S(1)} %copy-done, s32[1,512]{1,0:T(1,128)S(1)} %bitcast.3, f32[1,512]{1,0:T(1,128)S(1)} %bitcast.4), custom_call_target="tpu_custom_call" | custom-call | tf_op jit(solution)/shard_map/pallas_call | solution.py:441
  45.8 0.6 %copy.7 = f32[512]{0:T(512)} copy(f32[512]{0:T(512)S(1)} %bitcast.5) | data formatting | bytes 4096
  46.4 0.8 %copy.8 = f32[512,256]{1,0:T(8,128)} copy(f32[512,256]{1,0:T(8,128)S(1)} %get-tuple-element.9) | data formatting | bytes 1048576
Async XLA Ops:
  0.6 0.7 %copy-start.1 = (s32[512]{0:T(512)S(1)}, s32[512]{0:T(512)}, u32[]{:S(2)}) copy-start(s32[512]{0:T(512)} %param.4) | copy-start | bytes 6148
  1.3 0.9 %copy-start = (bf16[512,256]{1,0:T(8,128)(2,1)S(1)}, bf16[512,256]{1,0:T(8,128)(2,1)}, u32[]{:S(2)}) copy-start(bf16[512,256]{1,0:T(8,128)(2,1)} %views_ref.1) | copy-start | bytes 786436
  2.3 0.7 %copy-start.2 = (f32[512]{0:T(512)S(1)}, f32[512]{0:T(512)}, u32[]{:S(2)}) copy-start(f32[512]{0:T(512)} %param.5) | copy-start | bytes 6148
